TPU v7x, 256 devices: a whole 4x4x8 slice. The times are simulated.
256 devices in a mesh: fsdp: 32 (over x_lo, z, core), ctx: 8 (over y, x_hi).
Axes of the slice: x: 4 (x_hi: 2, x_lo: 2; x = x_hi * 2 + x_lo), y: 4, z: 8, core: 2. Of those that a mesh axis runs over, the one named last changes fastest.
Arguments:
- tokens: bfloat16 [32, 4096, 4096], P('fsdp', 'ctx'), may hold values from -24 to 24
- w_query: bfloat16 [4096, 2, 128], P('fsdp'), may hold values from -0.09375 to 0.09375
- w_key: bfloat16 [4096, 2, 128], P('fsdp'), may hold values from -0.09375 to 0.09375
- w_value: bfloat16 [4096, 2, 4, 128], P('fsdp'), may hold values from -0.09375 to 0.09375
- w_out: bfloat16 [2, 4, 128, 4096], P(None, None, None, 'fsdp'), may hold values from -0.5 to 0.5
- value_experts: int32 [32, 4096, 2, 2], P('fsdp', 'ctx'), may hold values from 0 to 3, all different within a row
- value_gates: bfloat16 [32, 4096, 2, 2], P('fsdp', 'ctx'), may hold values from 0.25 to 1
- output_experts: int32 [32, 4096, 2, 2], P('fsdp', 'ctx'), may hold values from 0 to 3, all different within a row
- output_gates: bfloat16 [32, 4096, 2, 2], P('fsdp', 'ctx'), may hold values from 0.25 to 1
Outputs:
- projected: bfloat16 [32, 4096, 4096], P('fsdp', 'ctx')
Inputs may be any that keep to these rules, and one draw needn't show every extreme that they name: `value_experts`: each token and head names 2 different experts. `output_experts`: each token and head names 2 different experts.
All inputs are finite; a program needn't handle non-finite values.
Results may differ from a plain program's by a relative error of at most 0.015.
The roundings to bfloat16 on the way count: a program that leaves them out, or rounds other values in their place, can miss the bound.
Values may be sent and summed in bfloat16 or wider, within the bound.
No kernel may reach another device: no remote copies, remote signals or barrier semaphores. Data moves between devices by JAX's collectives and lax.ppermute only.
A program may use at most 128 MiB of HBM per device.

v0:
```python
import math
import jax
import jax.numpy as jnp
from jax import lax
from jax.sharding import PartitionSpec as P


def passed_along(shard, axis, by):
    count = lax.axis_size(axis)
    pairs = [(i, i + by) for i in range(count) if 0 <= i + by < count]
    return lax.ppermute(shard, axis, pairs)


def expert_mix(indices, gates, experts):
    one_hot = (indices[..., None] == jnp.arange(experts, dtype=jnp.int32)).astype(jnp.float32)
    return jnp.sum(gates.astype(jnp.float32)[..., None] * one_hot, axis=-2)


def attend(totals, queries, key_rows, value_rows, query_pos, key_start):
    run_max, run_sum, run_acc = totals
    scores = jnp.einsum(
        "qhd,khd->hqk", queries, key_rows, preferred_element_type=jnp.float32
    ) / math.sqrt(queries.shape[2])
    key_pos = key_start + jnp.arange(key_rows.shape[0], dtype=jnp.int32)
    visible = (query_pos[:, None] >= key_pos[None, :])[None]
    scores = jnp.where(visible, scores, -jnp.inf)
    new_max = jnp.maximum(run_max, jnp.max(scores, axis=-1))
    rescale = jnp.exp(run_max - new_max)
    weights = jnp.exp(scores - new_max[..., None])
    run_sum = run_sum * rescale + jnp.sum(weights, axis=-1)
    update = jnp.einsum(
        "hqk,khd->qhd", weights.astype(jnp.bfloat16), value_rows, preferred_element_type=jnp.float32
    )
    run_acc = run_acc * jnp.transpose(rescale)[:, :, None] + update
    return (new_max, run_sum, run_acc)


def on_device(
    tokens, w_query, w_key, w_value, w_out, value_experts, value_gates, output_experts, output_gates
):
    tok_rows = tokens.shape[1]
    inputs = tokens[0]
    head_count = w_query.shape[1]
    head_dim = w_query.shape[2]
    experts = w_value.shape[2]
    pieces = (
        lax.all_gather(w_query, "fsdp", axis=0, tiled=True),
        lax.all_gather(w_key, "fsdp", axis=0, tiled=True),
        lax.all_gather(w_value, "fsdp", axis=0, tiled=True),
    )
    piece_rows = pieces[0].shape[0]
    query_sum, key_sum, value_sum = tuple(
        (
            jnp.dot(inputs, panel.reshape(piece_rows, -1), preferred_element_type=jnp.float32)
            for panel in pieces
        )
    )
    queries = query_sum.astype(jnp.bfloat16).reshape(tok_rows, head_count, head_dim)
    key_rows = key_sum.astype(jnp.bfloat16).reshape(tok_rows, head_count, head_dim)
    value_mix = expert_mix(value_experts[0], value_gates[0], experts)
    value_rows = jnp.sum(
        value_mix[..., None] * value_sum.reshape(tok_rows, head_count, experts, head_dim), axis=2
    ).astype(jnp.bfloat16)
    cycle_size = lax.axis_size("ctx")
    cycle_pos = lax.axis_index("ctx")
    query_pos = cycle_pos * tok_rows + jnp.arange(tok_rows, dtype=jnp.int32)
    start_state = (
        jnp.full((head_count, tok_rows), -1e30, jnp.float32),
        jnp.zeros((head_count, tok_rows), jnp.float32),
        jnp.zeros((tok_rows, head_count, head_dim), jnp.float32),
    )
    kv_block = jnp.stack([key_rows, value_rows])
    first_state = attend(
        start_state, queries, key_rows, value_rows, query_pos, cycle_pos * tok_rows
    )

    def cycle_step(passes, bundle):
        totals, moving = bundle
        moving = passed_along(moving, "ctx", 1)
        owner = cycle_pos - passes - 1
        key_start = jnp.where(owner >= 0, owner * tok_rows, cycle_size * tok_rows)
        totals = attend(totals, queries, moving[0], moving[1], query_pos, key_start)
        return (totals, moving)

    final_state, unused_block = lax.fori_loop(
        0, cycle_size - 1, cycle_step, (first_state, kv_block)
    )
    run_max, run_sum, run_acc = final_state
    attended = (run_acc / jnp.transpose(run_sum)[:, :, None]).astype(jnp.bfloat16)
    output_mix = expert_mix(output_experts[0], output_gates[0], experts).astype(jnp.bfloat16)
    mixed_in = (
        output_mix.astype(jnp.float32)[..., None] * attended.astype(jnp.float32)[:, :, None, :]
    ).astype(jnp.bfloat16)
    mixed_flat = mixed_in.reshape(tok_rows, head_count * experts * head_dim)
    panel_piece = lax.all_gather(w_out, "fsdp", axis=3, tiled=True)
    result = jnp.dot(
        mixed_flat,
        panel_piece.reshape(-1, panel_piece.shape[3]),
        preferred_element_type=jnp.float32,
    )
    return result.astype(jnp.bfloat16)[None]


def solution(mesh):
    in_specs = (
        P("fsdp", "ctx", None),
        P("fsdp", None, None),
        P("fsdp", None, None),
        P("fsdp", None, None, None),
        P(None, None, None, "fsdp"),
        P("fsdp", "ctx", None, None),
        P("fsdp", "ctx", None, None),
        P("fsdp", "ctx", None, None),
        P("fsdp", "ctx", None, None),
    )
    out_specs = P("fsdp", "ctx", None)
    return jax.shard_map(
        on_device, mesh=mesh, in_specs=in_specs, out_specs=out_specs, check_vma=False
    )
```

profile of v0, /device:TPU:248, one launch (start us, length us, event | category | flops | bytes accessed | tf_op | source)
XLA Modules:
  0.0 401.1 jit_solution(15075435414131235273)
XLA Ops:
  6.5 0.7 all-gather.7.cloned.1.call-update
  7.3 0.7 all-gather.5.cloned.1.call-update
  8.1 0.7 all-gather.9.cloned.1.call-update
  8.8 0.5 all-gather.11.cloned.1.call-update
  9.3 0.7 bitcast_convert_fusion.2
  10.0 0.7 select_reduce_fusion.1
  10.8 0.7 bitcast_convert_fusion.1
  11.4 0.7 select_reduce_fusion
  12.4 60.2 %all-gather.7.cloned.1.call-done = bf16[4096,2,128]{2,1,0:T(2,128)(2,1)} async-done(((bf16[128,2,128]{2,1,0:T(2,128)(2,1)}), bf16[4096,2,128]{2,1,0:T(2,128)(2,1)}) %all-gather.7.cloned.1.call-update) | async-done | bytes 2097168 | tf_op jit(solution)/shard_map/all_gather | solution.py:48
  72.6 4.2 %fusion.40 = bf16[512,256]{0,1:T(8,128)(2,1)S(1)} fusion(bf16[512,8,2,128]{3,2,1,0:T(2,128)(2,1)} %bitcast.103, bf16[1,512,4096]{2,1,0:T(8,128)(2,1)} %param.11), kind=kOutput, calls=%fused_computation.46 | convolution fusion | flops 1073872896 | bytes 6553600 | tf_op jit(solution)/shard_map/dot_general | solution.py:54
  76.9 61.9 %all-gather.5.cloned.1.call-done = bf16[4096,2,128]{2,1,0:T(2,128)(2,1)} async-done(((bf16[128,2,128]{2,1,0:T(2,128)(2,1)}), bf16[4096,2,128]{2,1,0:T(2,128)(2,1)}) %all-gather.5.cloned.1.call-update) | async-done | bytes 2097168 | tf_op jit(solution)/shard_map/all_gather | solution.py:47
  138.8 4.2 %fusion.35 = bf16[512,256]{0,1:T(8,128)(2,1)S(1)} fusion(bf16[512,8,2,128]{3,2,1,0:T(2,128)(2,1)} %bitcast.104, bf16[1,512,4096]{2,1,0:T(8,128)(2,1)} %param.11), kind=kOutput, calls=%fused_computation.45 | convolution fusion | flops 1073872896 | bytes 6553600 | tf_op jit(solution)/shard_map/dot_general | solution.py:54
  143.2 0.6 fusion.27
  144.3 68.5 %all-gather.9.cloned.1.call-done = bf16[4096,2,4,128]{3,2,1,0:T(4,128)(2,1)} async-done(((bf16[128,2,4,128]{3,2,1,0:T(4,128)(2,1)}), bf16[4096,2,4,128]{3,2,1,0:T(4,128)(2,1)}) %all-gather.9.cloned.1.call-update) | async-done | bytes 8388624 | tf_op jit(solution)/shard_map/all_gather | solution.py:49
  212.8 13.8 %copy.52 = bf16[4096,2,4,128]{0,3,2,1:T(8,128)(2,1)} copy(bf16[4096,2,4,128]{3,2,1,0:T(4,128)(2,1)} %all-gather.9.cloned.1.call-done) | data formatting | bytes 16777216 | tf_op jit(solution)/shard_map/reshape | solution.py:54
  226.7 9.1 %multiply_reduce_fusion = bf16[512,2,128]{2,0,1:T(8,128)(2,1)} fusion(bf16[4096,2,4,128]{0,3,2,1:T(8,128)(2,1)} %copy.52, bf16[1,512,4096]{2,1,0:T(8,128)(2,1)} %param.11, f32[512,2,4]{0,2,1:T(4,128)S(1)} %select_reduce_fusion), kind=kOutput, calls=%fused_computation.37 | convolution fusion | flops 4295884800 | bytes 12861440 | tf_op jit(solution)/shard_map/dot_general | solution.py:54
  235.8 1.7 fusion.34
  237.7 1.0 pad_maximum_fusion
  238.7 147.3 %while.22 = (s32[]{:T(128)}, f32[2,512]{1,0:T(2,128)S(1)}, f32[2,512]{1,0:T(2,128)S(1)}, f32[512,2,128]{2,0,1:T(8,128)S(1)}, bf16[2,512,2,128]{3,1,2,0:T(8,128)(...) while((s32[]{:T(128)}, f32[2,512]{1,0:T(2,128)S(1)}, ...), condition=%wide.region_8.9_spmd.clone, body=%wide.region_5.8_spmd.clone.sunk | while | flops 274731008 | bytes 12394735 | solution.py:85
  238.7 4.9 %collective-permute-start = (bf16[2,512,2,128]{3,1,2,0:T(8,128)(2,1)S(1)}, bf16[2,512,2,128]{3,1,2,0:T(8,128)(2,1)S(1)}, u32[]{:S(2)}, u32[]{:S(2)}) collective-permute-start(bf16[2,512,2,128]{3,1,2,0:T(8,128)(2,1)S(1)} %get-tuple-element.353), channel_id=1, source_target_pairs={{0,1},{1,2},{2,3},{3,4},{4,5},{5,6},{6,7},{8,9},{9,10},{10,11},{11... | collective-permute-start | bytes 1572872 | tf_op jit(solution)/shard_map/while/body/eval_jaxpr/ppermute | solution.py:11
  243.8 22.6 %collective-permute-done = bf16[2,512,2,128]{3,1,2,0:T(8,128)(2,1)S(1)} collective-permute-done((bf16[2,512,2,128]{3,1,2,0:T(8,128)(2,1)S(1)}, bf16[2,512,2,128]{3,1,2,0:T(8,128)(2,1)S(1)}, u32[]{:S(2)}, u32[]{:S(2)}) %collective-permute-start) | collective-permute-done | bytes 524320 | tf_op jit(solution)/shard_map/while/body/eval_jaxpr/ppermute | solution.py:11
  266.5 0.5 fusion.71
  267.6 1.0 fusion.74
  268.6 2.6 collective-permute-start
  271.5 25.0 %collective-permute-done = bf16[2,512,2,128]{3,1,2,0:T(8,128)(2,1)S(1)} collective-permute-done((bf16[2,512,2,128]{3,1,2,0:T(8,128)(2,1)S(1)}, bf16[2,512,2,128]{3,1,2,0:T(8,128)(2,1)S(1)}, u32[]{:S(2)}, u32[]{:S(2)}) %collective-permute-start) | collective-permute-done | bytes 524320 | tf_op jit(solution)/shard_map/while/body/eval_jaxpr/ppermute | solution.py:11
  296.5 0.5 fusion.71
  297.7 1.0 fusion.74
  298.7 2.0 collective-permute-start
  300.9 16.0 %collective-permute-done = bf16[2,512,2,128]{3,1,2,0:T(8,128)(2,1)S(1)} collective-permute-done((bf16[2,512,2,128]{3,1,2,0:T(8,128)(2,1)S(1)}, bf16[2,512,2,128]{3,1,2,0:T(8,128)(2,1)S(1)}, u32[]{:S(2)}, u32[]{:S(2)}) %collective-permute-start) | collective-permute-done | bytes 524320 | tf_op jit(solution)/shard_map/while/body/eval_jaxpr/ppermute | solution.py:11
  316.9 0.5 fusion.71
  318.0 1.0 fusion.74
  319.0 3.4 collective-permute-start
  322.7 12.2 %collective-permute-done = bf16[2,512,2,128]{3,1,2,0:T(8,128)(2,1)S(1)} collective-permute-done((bf16[2,512,2,128]{3,1,2,0:T(8,128)(2,1)S(1)}, bf16[2,512,2,128]{3,1,2,0:T(8,128)(2,1)S(1)}, u32[]{:S(2)}, u32[]{:S(2)}) %collective-permute-start) | collective-permute-done | bytes 524320 | tf_op jit(solution)/shard_map/while/body/eval_jaxpr/ppermute | solution.py:11
  334.9 0.5 fusion.71
  336.1 1.0 fusion.74
  337.0 3.7 collective-permute-start
  341.0 11.0 %collective-permute-done = bf16[2,512,2,128]{3,1,2,0:T(8,128)(2,1)S(1)} collective-permute-done((bf16[2,512,2,128]{3,1,2,0:T(8,128)(2,1)S(1)}, bf16[2,512,2,128]{3,1,2,0:T(8,128)(2,1)S(1)}, u32[]{:S(2)}, u32[]{:S(2)}) %collective-permute-start) | collective-permute-done | bytes 524320 | tf_op jit(solution)/shard_map/while/body/eval_jaxpr/ppermute | solution.py:11
  352.0 0.5 fusion.71
  353.2 1.0 fusion.74
  354.2 4.0 collective-permute-start
  358.4 9.9 %collective-permute-done = bf16[2,512,2,128]{3,1,2,0:T(8,128)(2,1)S(1)} collective-permute-done((bf16[2,512,2,128]{3,1,2,0:T(8,128)(2,1)S(1)}, bf16[2,512,2,128]{3,1,2,0:T(8,128)(2,1)S(1)}, u32[]{:S(2)}, u32[]{:S(2)}) %collective-permute-start) | collective-permute-done | bytes 524320 | tf_op jit(solution)/shard_map/while/body/eval_jaxpr/ppermute | solution.py:11
  368.2 0.5 fusion.71
  369.4 1.0 fusion.74
  370.4 4.2 %collective-permute-start = (bf16[2,512,2,128]{3,1,2,0:T(8,128)(2,1)S(1)}, bf16[2,512,2,128]{3,1,2,0:T(8,128)(2,1)S(1)}, u32[]{:S(2)}, u32[]{:S(2)}) collective-permute-start(bf16[2,512,2,128]{3,1,2,0:T(8,128)(2,1)S(1)} %get-tuple-element.353), channel_id=1, source_target_pairs={{0,1},{1,2},{2,3},{3,4},{4,5},{5,6},{6,7},{8,9},{9,10},{10,11},{11... | collective-permute-start | bytes 1572872 | tf_op jit(solution)/shard_map/while/body/eval_jaxpr/ppermute | solution.py:11
  374.8 9.0 %collective-permute-done = bf16[2,512,2,128]{3,1,2,0:T(8,128)(2,1)S(1)} collective-permute-done((bf16[2,512,2,128]{3,1,2,0:T(8,128)(2,1)S(1)}, bf16[2,512,2,128]{3,1,2,0:T(8,128)(2,1)S(1)}, u32[]{:S(2)}, u32[]{:S(2)}) %collective-permute-start) | collective-permute-done | bytes 524320 | tf_op jit(solution)/shard_map/while/body/eval_jaxpr/ppermute | solution.py:11
  383.8 0.5 fusion.71
  385.0 1.0 fusion.74
  386.2 8.3 %fusion.17 = bf16[1,512,4096]{2,1,0:T(8,128)(2,1)} fusion(bf16[2,4,128,4096]{3,2,1,0:T(8,128)(2,1)} %all-gather.11.cloned.1.call-done, f32[512,2,128]{2,0,1:T(8,128)S(1)} %fusion.52, f32[512,2,4]{0,2,1:T(4,128)S(1)} %convert_element_type.118), kind=kOutput, calls=%fused_computation.26 | convolution fusion | flops 4298113024 | bytes 13123584 | tf_op jit(solution)/shard_map/dot_general | solution.py:96
  (64 shorter events, 7.1 us)
Async XLA Ops:
  6.5 66.0 %all-gather.7.cloned.1.call-start = ((), (), s32[]{:S(2)}) async-start(), calls=%async_computation.1 | async-start | bytes 2162688 | tf_op jit(solution)/shard_map/all_gather | solution.py:48
  7.3 131.6 %all-gather.5.cloned.1.call-start = ((), (), s32[]{:S(2)}) async-start(), calls=%async_computation | async-start | bytes 2162688 | tf_op jit(solution)/shard_map/all_gather | solution.py:47
  8.0 204.8 %all-gather.9.cloned.1.call-start = ((), (), s32[]{:S(2)}) async-start(), calls=%async_computation.2 | async-start | bytes 8650752 | tf_op jit(solution)/shard_map/all_gather | solution.py:49
  8.7 377.5 %all-gather.11.cloned.1.call-start = ((), (), s32[]{:S(2)}) async-start(), calls=%async_computation.3 | async-start | bytes 8650752 | tf_op jit(solution)/shard_map/all_gather | solution.py:95
  238.7 27.8 %collective-permute-start = (bf16[2,512,2,128]{3,1,2,0:T(8,128)(2,1)S(1)}, bf16[2,512,2,128]{3,1,2,0:T(8,128)(2,1)S(1)}, u32[]{:S(2)}, u32[]{:S(2)}) collective-permute-start(bf16[2,512,2,128]{3,1,2,0:T(8,128)(2,1)S(1)} %get-tuple-element.353), channel_id=1, source_target_pairs={{0,1},{1,2},{2,3},{3,4},{4,5},{5,6},{6,7},{8,9},{9,10},{10,11},{11... | collective-permute-start | bytes 1572872 | tf_op jit(solution)/shard_map/while/body/eval_jaxpr/ppermute | solution.py:11
  268.6 27.9 %collective-permute-start = (bf16[2,512,2,128]{3,1,2,0:T(8,128)(2,1)S(1)}, bf16[2,512,2,128]{3,1,2,0:T(8,128)(2,1)S(1)}, u32[]{:S(2)}, u32[]{:S(2)}) collective-permute-start(bf16[2,512,2,128]{3,1,2,0:T(8,128)(2,1)S(1)} %get-tuple-element.353), channel_id=1, source_target_pairs={{0,1},{1,2},{2,3},{3,4},{4,5},{5,6},{6,7},{8,9},{9,10},{10,11},{11... | collective-permute-start | bytes 1572872 | tf_op jit(solution)/shard_map/while/body/eval_jaxpr/ppermute | solution.py:11
  298.7 18.2 %collective-permute-start = (bf16[2,512,2,128]{3,1,2,0:T(8,128)(2,1)S(1)}, bf16[2,512,2,128]{3,1,2,0:T(8,128)(2,1)S(1)}, u32[]{:S(2)}, u32[]{:S(2)}) collective-permute-start(bf16[2,512,2,128]{3,1,2,0:T(8,128)(2,1)S(1)} %get-tuple-element.353), channel_id=1, source_target_pairs={{0,1},{1,2},{2,3},{3,4},{4,5},{5,6},{6,7},{8,9},{9,10},{10,11},{11... | collective-permute-start | bytes 1572872 | tf_op jit(solution)/shard_map/while/body/eval_jaxpr/ppermute | solution.py:11
  319.0 15.9 %collective-permute-start = (bf16[2,512,2,128]{3,1,2,0:T(8,128)(2,1)S(1)}, bf16[2,512,2,128]{3,1,2,0:T(8,128)(2,1)S(1)}, u32[]{:S(2)}, u32[]{:S(2)}) collective-permute-start(bf16[2,512,2,128]{3,1,2,0:T(8,128)(2,1)S(1)} %get-tuple-element.353), channel_id=1, source_target_pairs={{0,1},{1,2},{2,3},{3,4},{4,5},{5,6},{6,7},{8,9},{9,10},{10,11},{11... | collective-permute-start | bytes 1572872 | tf_op jit(solution)/shard_map/while/body/eval_jaxpr/ppermute | solution.py:11
  337.0 15.0 %collective-permute-start = (bf16[2,512,2,128]{3,1,2,0:T(8,128)(2,1)S(1)}, bf16[2,512,2,128]{3,1,2,0:T(8,128)(2,1)S(1)}, u32[]{:S(2)}, u32[]{:S(2)}) collective-permute-start(bf16[2,512,2,128]{3,1,2,0:T(8,128)(2,1)S(1)} %get-tuple-element.353), channel_id=1, source_target_pairs={{0,1},{1,2},{2,3},{3,4},{4,5},{5,6},{6,7},{8,9},{9,10},{10,11},{11... | collective-permute-start | bytes 1572872 | tf_op jit(solution)/shard_map/while/body/eval_jaxpr/ppermute | solution.py:11
  354.2 14.1 %collective-permute-start = (bf16[2,512,2,128]{3,1,2,0:T(8,128)(2,1)S(1)}, bf16[2,512,2,128]{3,1,2,0:T(8,128)(2,1)S(1)}, u32[]{:S(2)}, u32[]{:S(2)}) collective-permute-start(bf16[2,512,2,128]{3,1,2,0:T(8,128)(2,1)S(1)} %get-tuple-element.353), channel_id=1, source_target_pairs={{0,1},{1,2},{2,3},{3,4},{4,5},{5,6},{6,7},{8,9},{9,10},{10,11},{11... | collective-permute-start | bytes 1572872 | tf_op jit(solution)/shard_map/while/body/eval_jaxpr/ppermute | solution.py:11
  370.4 13.5 %collective-permute-start = (bf16[2,512,2,128]{3,1,2,0:T(8,128)(2,1)S(1)}, bf16[2,512,2,128]{3,1,2,0:T(8,128)(2,1)S(1)}, u32[]{:S(2)}, u32[]{:S(2)}) collective-permute-start(bf16[2,512,2,128]{3,1,2,0:T(8,128)(2,1)S(1)} %get-tuple-element.353), channel_id=1, source_target_pairs={{0,1},{1,2},{2,3},{3,4},{4,5},{5,6},{6,7},{8,9},{9,10},{10,11},{11... | collective-permute-start | bytes 1572872 | tf_op jit(solution)/shard_map/while/body/eval_jaxpr/ppermute | solution.py:11
Sparse Core Ops, SparseCore 0:
  9.2 63.2 all-gather.6
  74.4 64.3 all-gather.4
  140.7 72.0 all-gather.8
  214.4 96.4 all-gather.10
where the time goes:
time: 402 us; the launch traced here: 401 us
  waiting for transfers between devices  299 us (74%)
  matrix products  38.6 us (10%)
  starting transfers between devices  25 us (6%)
  local copies, waits for them, and re-layouts  14.6 us (4%)
  between operations  13.2 us (3%)
  other arithmetic  9.98 us (2%)
    ppermute x7, waiting for transfers between devices, passed_along(): return lax.ppermute(shard, axis, pairs)  106 us
    all_gather x1, waiting for transfers between devices, on_device(): lax.all_gather(w_value, 'fsdp', axis=0, tiled=True)  68.5 us
    all_gather x1, waiting for transfers between devices, on_device(): lax.all_gather(w_query, 'fsdp', axis=0, tiled=True)  61.9 us
    all_gather x1, waiting for transfers between devices, on_device(): lax.all_gather(w_key, 'fsdp', axis=0, tiled=True)  60.2 us
    ppermute x7, starting transfers between devices, passed_along(): return lax.ppermute(shard, axis, pairs)  24.9 us
    dot_general x3, matrix products, on_device(): jnp.dot(inputs, panel.reshape(piece_rows, -1), preferred_element_type=jnp...  17.4 us
    reshape x1, local copies, waits for them, and re-layouts, on_device(): panel.reshape(piece_rows, -1)  13.8 us
    dot_general x8, matrix products, attend(): jnp.einsum('hqk,khd->qhd', weights.astype(jnp.bfloat16), value_rows, pref...  8.41 us
  transfers between devices with their start and end apart: 11, of which 10 were waited for; matrix products, arithmetic and copies ran while one was open for 14% of the time, Pallas kernels for 0%

commit v1 on v0

--- a/solution.py
+++ b/solution.py
@@ -44,7 +44,15 @@
     head_dim = w_query.shape[2]
     experts = w_value.shape[2]
     pieces = (
-        lax.all_gather(w_query, "fsdp", axis=0, tiled=True),
+        jnp.concatenate(
+            lax.all_to_all(
+                jnp.stack([w_query for _ in range(lax.axis_size("fsdp"))], 0),
+                axis_name="fsdp",
+                split_axis=0,
+                concat_axis=0,
+            ),
+            axis=0,
+        ),
         lax.all_gather(w_key, "fsdp", axis=0, tiled=True),
         lax.all_gather(w_value, "fsdp", axis=0, tiled=True),
     )

time: 402 us -> 352 us (0.88)
  waiting for transfers between devices: 299 us -> 243 us
  starting transfers between devices: 25 us -> 29.7 us
    all_gather x1 -> x0, waiting for transfers between devices: 61.9 us -> none  [on_device(): lax.all_gather(w_query, 'fsdp', axis=0, tiled=True)]
    all_to_all x0 -> x1, starting transfers between devices: none -> 7.08 us  [on_device(): lax.all_to_all(jnp.stack([w_query for _ in range(lax.axis_size('fsdp'))],...]
    ppermute x7, waiting for transfers between devices: 106 us -> 110 us  [passed_along(): return lax.ppermute(shard, axis, pairs)]
    all_gather x1, waiting for transfers between devices: 60.2 us -> 64.5 us  [on_device(): lax.all_gather(w_key, 'fsdp', axis=0, tiled=True)]
    another operation x0 -> x1, local copies, waits for them, and re-layouts: none -> 4.05 us  [on_device(): jnp.stack([w_query for _ in range(lax.axis_size('fsdp'))], 0)]
  transfers between devices with their start and end apart: 11 -> 11, of which waited for: 10 -> 9; matrix products, arithmetic and copies ran while one was open for 14% -> 16% of each run, Pallas kernels for 0% -> 0%
where the time goes in v1:
time: 352 us; the launch traced here: 351 us
  waiting for transfers between devices  243 us (69%)
  matrix products  37.9 us (11%)
  starting transfers between devices  29.7 us (8%)
  local copies, waits for them, and re-layouts  18.6 us (5%)
  between operations  13.3 us (4%)
  other arithmetic  7.22 us (2%)
    ppermute x7, waiting for transfers between devices, passed_along(): return lax.ppermute(shard, axis, pairs)  110 us
    all_gather x1, waiting for transfers between devices, on_device(): lax.all_gather(w_value, 'fsdp', axis=0, tiled=True)  66.3 us
    all_gather x1, waiting for transfers between devices, on_device(): lax.all_gather(w_key, 'fsdp', axis=0, tiled=True)  64.5 us
    ppermute x7, starting transfers between devices, passed_along(): return lax.ppermute(shard, axis, pairs)  22.6 us
    dot_general x3, matrix products, on_device(): jnp.dot(inputs, panel.reshape(piece_rows, -1), preferred_element_type=jnp...  16.8 us
    reshape x1, local copies, waits for them, and re-layouts, on_device(): panel.reshape(piece_rows, -1)  13.8 us
    dot_general x8, matrix products, attend(): jnp.einsum('hqk,khd->qhd', weights.astype(jnp.bfloat16), value_rows, pref...  8.41 us
    dot_general x1, matrix products, on_device(): jnp.dot(mixed_flat, panel_piece.reshape(-1, panel_piece.shape[3]), prefer...  8.32 us
  transfers between devices with their start and end apart: 11, of which 9 were waited for; matrix products, arithmetic and copies ran while one was open for 16% of the time, Pallas kernels for 0%

profile of v1, /device:TPU:248, one launch (start us, length us, event | category | flops | bytes accessed | tf_op | source)
XLA Modules:
  0.0 350.6 jit_solution(2102176849414516956)
XLA Ops:
  6.5 0.7 all-gather.4.cloned.1.call-update
  7.3 0.7 all-gather.6.cloned.1.call-update
  8.0 4.0 %stack.4 = bf16[32,128,2,128]{3,2,1,0:T(2,128)(2,1)} broadcast(bf16[128,2,128]{2,1,0:T(2,128)(2,1)} %param.12), dimensions={1,2,3} | broadcast | bytes 2162688 | tf_op jit(solution)/shard_map/stack | solution.py:49
  12.1 7.1 %all-to-all-start = ((bf16[32,128,2,128]{3,2,1,0:T(2,128)(2,1)}), bf16[32,128,2,128]{3,2,1,0:T(2,128)(2,1)S(1)}, u32[]{:S(2)}, u32[]{:S(2)}) async-start(bf16[32,128,2,128]{3,2,1,0:T(2,128)(2,1)} %stack.4), calls=%async_computation | async-start | bytes 4194304 | tf_op jit(solution)/shard_map/all_to_all | solution.py:48
  19.2 0.7 all-gather.8.cloned.1.call-update
  20.3 64.5 %all-gather.4.cloned.1.call-done = bf16[4096,2,128]{2,1,0:T(2,128)(2,1)} async-done(((bf16[128,2,128]{2,1,0:T(2,128)(2,1)}), bf16[4096,2,128]{2,1,0:T(2,128)(2,1)}) %all-gather.4.cloned.1.call-update) | async-done | bytes 2097168 | tf_op jit(solution)/shard_map/all_gather | solution.py:56
  84.8 4.2 %fusion.40 = bf16[512,256]{0,1:T(8,128)(2,1)S(1)} fusion(bf16[512,8,2,128]{3,2,1,0:T(2,128)(2,1)} %bitcast.105, bf16[1,512,4096]{2,1,0:T(8,128)(2,1)} %param.11), kind=kOutput, calls=%fused_computation.46 | convolution fusion | flops 1073872896 | bytes 6553600 | tf_op jit(solution)/shard_map/dot_general | solution.py:62
  89.1 3.5 fusion.35
  92.8 0.6 fusion.27
  93.4 0.5 fusion.33
  94.0 66.3 %all-gather.6.cloned.1.call-done = bf16[4096,2,4,128]{3,2,1,0:T(4,128)(2,1)} async-done(((bf16[128,2,4,128]{3,2,1,0:T(4,128)(2,1)}), bf16[4096,2,4,128]{3,2,1,0:T(4,128)(2,1)}) %all-gather.6.cloned.1.call-update) | async-done | bytes 8388624 | tf_op jit(solution)/shard_map/all_gather | solution.py:57
  160.3 13.8 %copy.52 = bf16[4096,2,4,128]{0,3,2,1:T(8,128)(2,1)} copy(bf16[4096,2,4,128]{3,2,1,0:T(4,128)(2,1)} %all-gather.6.cloned.1.call-done) | data formatting | bytes 16777216 | tf_op jit(solution)/shard_map/reshape | solution.py:62
  174.1 9.2 %multiply_reduce_fusion = bf16[512,2,128]{2,0,1:T(8,128)(2,1)} fusion(bf16[4096,2,4,128]{0,3,2,1:T(8,128)(2,1)} %copy.52, bf16[1,512,4096]{2,1,0:T(8,128)(2,1)} %param.11, f32[512,2,4]{0,2,1:T(4,128)S(1)} %select_reduce_fusion), kind=kOutput, calls=%fused_computation.37 | convolution fusion | flops 4295884800 | bytes 12861440 | tf_op jit(solution)/shard_map/dot_general | solution.py:62
  183.2 1.7 fusion.34
  185.1 1.0 pad_maximum_fusion
  186.1 149.4 %while.22 = (s32[]{:T(128)}, f32[2,512]{1,0:T(2,128)S(1)}, f32[2,512]{1,0:T(2,128)S(1)}, f32[512,2,128]{2,0,1:T(8,128)S(1)}, bf16[2,512,2,128]{3,1,2,0:T(8,128)(...) while((s32[]{:T(128)}, f32[2,512]{1,0:T(2,128)S(1)}, ...), condition=%wide.region_8.9_spmd.clone, body=%wide.region_5.8_spmd.clone.sunk | while | flops 274731008 | bytes 12394735 | solution.py:93
  186.1 4.9 %collective-permute-start = (bf16[2,512,2,128]{3,1,2,0:T(8,128)(2,1)S(1)}, bf16[2,512,2,128]{3,1,2,0:T(8,128)(2,1)S(1)}, u32[]{:S(2)}, u32[]{:S(2)}) collective-permute-start(bf16[2,512,2,128]{3,1,2,0:T(8,128)(2,1)S(1)} %get-tuple-element.353), channel_id=1, source_target_pairs={{0,1},{1,2},{2,3},{3,4},{4,5},{5,6},{6,7},{8,9},{9,10},{10,11},{11... | collective-permute-start | bytes 1572872 | tf_op jit(solution)/shard_map/while/body/eval_jaxpr/ppermute | solution.py:11
  191.2 21.9 %collective-permute-done = bf16[2,512,2,128]{3,1,2,0:T(8,128)(2,1)S(1)} collective-permute-done((bf16[2,512,2,128]{3,1,2,0:T(8,128)(2,1)S(1)}, bf16[2,512,2,128]{3,1,2,0:T(8,128)(2,1)S(1)}, u32[]{:S(2)}, u32[]{:S(2)}) %collective-permute-start) | collective-permute-done | bytes 524320 | tf_op jit(solution)/shard_map/while/body/eval_jaxpr/ppermute | solution.py:11
  213.1 0.5 fusion.71
  213.7 0.5 fusion.73
  214.2 1.0 fusion.74
  215.2 3.2 collective-permute-start
  218.7 25.2 %collective-permute-done = bf16[2,512,2,128]{3,1,2,0:T(8,128)(2,1)S(1)} collective-permute-done((bf16[2,512,2,128]{3,1,2,0:T(8,128)(2,1)S(1)}, bf16[2,512,2,128]{3,1,2,0:T(8,128)(2,1)S(1)}, u32[]{:S(2)}, u32[]{:S(2)}) %collective-permute-start) | collective-permute-done | bytes 524320 | tf_op jit(solution)/shard_map/while/body/eval_jaxpr/ppermute | solution.py:11
  243.9 0.5 fusion.71
  244.5 0.5 fusion.73
  245.1 1.0 fusion.74
  246.1 2.3 collective-permute-start
  248.6 16.2 %collective-permute-done = bf16[2,512,2,128]{3,1,2,0:T(8,128)(2,1)S(1)} collective-permute-done((bf16[2,512,2,128]{3,1,2,0:T(8,128)(2,1)S(1)}, bf16[2,512,2,128]{3,1,2,0:T(8,128)(2,1)S(1)}, u32[]{:S(2)}, u32[]{:S(2)}) %collective-permute-start) | collective-permute-done | bytes 524320 | tf_op jit(solution)/shard_map/while/body/eval_jaxpr/ppermute | solution.py:11
  264.8 0.5 fusion.71
  265.4 0.5 fusion.73
  265.9 1.0 fusion.74
  266.9 3.2 collective-permute-start
  270.4 12.9 %collective-permute-done = bf16[2,512,2,128]{3,1,2,0:T(8,128)(2,1)S(1)} collective-permute-done((bf16[2,512,2,128]{3,1,2,0:T(8,128)(2,1)S(1)}, bf16[2,512,2,128]{3,1,2,0:T(8,128)(2,1)S(1)}, u32[]{:S(2)}, u32[]{:S(2)}) %collective-permute-start) | collective-permute-done | bytes 524320 | tf_op jit(solution)/shard_map/while/body/eval_jaxpr/ppermute | solution.py:11
  283.3 0.5 fusion.71
  284.5 1.0 fusion.74
  285.5 3.1 collective-permute-start
  288.8 12.1 %collective-permute-done = bf16[2,512,2,128]{3,1,2,0:T(8,128)(2,1)S(1)} collective-permute-done((bf16[2,512,2,128]{3,1,2,0:T(8,128)(2,1)S(1)}, bf16[2,512,2,128]{3,1,2,0:T(8,128)(2,1)S(1)}, u32[]{:S(2)}, u32[]{:S(2)}) %collective-permute-start) | collective-permute-done | bytes 524320 | tf_op jit(solution)/shard_map/while/body/eval_jaxpr/ppermute | solution.py:11
  300.9 0.5 fusion.71
  302.1 1.0 fusion.74
  303.1 3.0 collective-permute-start
  306.3 11.4 %collective-permute-done = bf16[2,512,2,128]{3,1,2,0:T(8,128)(2,1)S(1)} collective-permute-done((bf16[2,512,2,128]{3,1,2,0:T(8,128)(2,1)S(1)}, bf16[2,512,2,128]{3,1,2,0:T(8,128)(2,1)S(1)}, u32[]{:S(2)}, u32[]{:S(2)}) %collective-permute-start) | collective-permute-done | bytes 524320 | tf_op jit(solution)/shard_map/while/body/eval_jaxpr/ppermute | solution.py:11
  317.6 0.5 fusion.71
  318.8 1.0 fusion.74
  319.8 2.8 collective-permute-start
  322.8 10.6 %collective-permute-done = bf16[2,512,2,128]{3,1,2,0:T(8,128)(2,1)S(1)} collective-permute-done((bf16[2,512,2,128]{3,1,2,0:T(8,128)(2,1)S(1)}, bf16[2,512,2,128]{3,1,2,0:T(8,128)(2,1)S(1)}, u32[]{:S(2)}, u32[]{:S(2)}) %collective-permute-start) | collective-permute-done | bytes 524320 | tf_op jit(solution)/shard_map/while/body/eval_jaxpr/ppermute | solution.py:11
  333.4 0.5 fusion.71
  334.5 1.0 fusion.74
  335.8 8.3 %fusion.17 = bf16[1,512,4096]{2,1,0:T(8,128)(2,1)} fusion(bf16[2,4,128,4096]{3,2,1,0:T(8,128)(2,1)} %all-gather.8.cloned.1.call-done, f32[512,2,128]{2,0,1:T(8,128)S(1)} %fusion.52, f32[512,2,4]{0,2,1:T(4,128)S(1)} %convert_element_type.118), kind=kOutput, calls=%fused_computation.26 | convolution fusion | flops 4298113024 | bytes 13123584 | tf_op jit(solution)/shard_map/dot_general | solution.py:104
  (72 shorter events, 5.1 us)
Async XLA Ops:
  6.5 78.2 %all-gather.4.cloned.1.call-start = ((), (), s32[]{:S(2)}) async-start(), calls=%async_computation.1 | async-start | bytes 2162688 | tf_op jit(solution)/shard_map/all_gather | solution.py:56
  7.3 153.0 %all-gather.6.cloned.1.call-start = ((), (), s32[]{:S(2)}) async-start(), calls=%async_computation.2 | async-start | bytes 8650752 | tf_op jit(solution)/shard_map/all_gather | solution.py:57
  12.1 7.8 %copy-start.2 = (bf16[1,512,2,2]{1,3,2,0:T(2,128)(2,1)S(1)}, bf16[1,512,2,2]{1,3,2,0:T(2,128)(2,1)}, u32[]{:S(2)}) copy-start(bf16[1,512,2,2]{1,3,2,0:T(2,128)(2,1)} %param.19) | copy-start | bytes 12292
  12.1 7.9 %copy-start = (s32[1,512,2,2]{1,3,2,0:T(2,128)S(1)}, s32[1,512,2,2]{1,3,2,0:T(2,128)}, u32[]{:S(2)}) copy-start(s32[1,512,2,2]{1,3,2,0:T(2,128)} %param.18) | copy-start | bytes 24580
  12.1 7.9 %copy-start.3 = (bf16[1,512,2,2]{1,3,2,0:T(2,128)(2,1)S(1)}, bf16[1,512,2,2]{1,3,2,0:T(2,128)(2,1)}, u32[]{:S(2)}) copy-start(bf16[1,512,2,2]{1,3,2,0:T(2,128)(2,1)} %param.17) | copy-start | bytes 12292
  12.1 7.9 %copy-start.1 = (s32[1,512,2,2]{1,3,2,0:T(2,128)S(1)}, s32[1,512,2,2]{1,3,2,0:T(2,128)}, u32[]{:S(2)}) copy-start(s32[1,512,2,2]{1,3,2,0:T(2,128)} %param.16) | copy-start | bytes 24580
  12.1 77.1 %all-to-all-start = ((bf16[32,128,2,128]{3,2,1,0:T(2,128)(2,1)}), bf16[32,128,2,128]{3,2,1,0:T(2,128)(2,1)S(1)}, u32[]{:S(2)}, u32[]{:S(2)}) async-start(bf16[32,128,2,128]{3,2,1,0:T(2,128)(2,1)} %stack.4), calls=%async_computation | async-start | bytes 4194304 | tf_op jit(solution)/shard_map/all_to_all | solution.py:48
  19.1 316.6 %all-gather.8.cloned.1.call-start = ((), (), s32[]{:S(2)}) async-start(), calls=%async_computation.3 | async-start | bytes 8650752 | tf_op jit(solution)/shard_map/all_gather | solution.py:103
  186.1 27.0 %collective-permute-start = (bf16[2,512,2,128]{3,1,2,0:T(8,128)(2,1)S(1)}, bf16[2,512,2,128]{3,1,2,0:T(8,128)(2,1)S(1)}, u32[]{:S(2)}, u32[]{:S(2)}) collective-permute-start(bf16[2,512,2,128]{3,1,2,0:T(8,128)(2,1)S(1)} %get-tuple-element.353), channel_id=1, source_target_pairs={{0,1},{1,2},{2,3},{3,4},{4,5},{5,6},{6,7},{8,9},{9,10},{10,11},{11... | collective-permute-start | bytes 1572872 | tf_op jit(solution)/shard_map/while/body/eval_jaxpr/ppermute | solution.py:11
  215.2 28.7 %collective-permute-start = (bf16[2,512,2,128]{3,1,2,0:T(8,128)(2,1)S(1)}, bf16[2,512,2,128]{3,1,2,0:T(8,128)(2,1)S(1)}, u32[]{:S(2)}, u32[]{:S(2)}) collective-permute-start(bf16[2,512,2,128]{3,1,2,0:T(8,128)(2,1)S(1)} %get-tuple-element.353), channel_id=1, source_target_pairs={{0,1},{1,2},{2,3},{3,4},{4,5},{5,6},{6,7},{8,9},{9,10},{10,11},{11... | collective-permute-start | bytes 1572872 | tf_op jit(solution)/shard_map/while/body/eval_jaxpr/ppermute | solution.py:11
  246.1 18.7 %collective-permute-start = (bf16[2,512,2,128]{3,1,2,0:T(8,128)(2,1)S(1)}, bf16[2,512,2,128]{3,1,2,0:T(8,128)(2,1)S(1)}, u32[]{:S(2)}, u32[]{:S(2)}) collective-permute-start(bf16[2,512,2,128]{3,1,2,0:T(8,128)(2,1)S(1)} %get-tuple-element.353), channel_id=1, source_target_pairs={{0,1},{1,2},{2,3},{3,4},{4,5},{5,6},{6,7},{8,9},{9,10},{10,11},{11... | collective-permute-start | bytes 1572872 | tf_op jit(solution)/shard_map/while/body/eval_jaxpr/ppermute | solution.py:11
  266.9 16.4 %collective-permute-start = (bf16[2,512,2,128]{3,1,2,0:T(8,128)(2,1)S(1)}, bf16[2,512,2,128]{3,1,2,0:T(8,128)(2,1)S(1)}, u32[]{:S(2)}, u32[]{:S(2)}) collective-permute-start(bf16[2,512,2,128]{3,1,2,0:T(8,128)(2,1)S(1)} %get-tuple-element.353), channel_id=1, source_target_pairs={{0,1},{1,2},{2,3},{3,4},{4,5},{5,6},{6,7},{8,9},{9,10},{10,11},{11... | collective-permute-start | bytes 1572872 | tf_op jit(solution)/shard_map/while/body/eval_jaxpr/ppermute | solution.py:11
  285.5 15.5 %collective-permute-start = (bf16[2,512,2,128]{3,1,2,0:T(8,128)(2,1)S(1)}, bf16[2,512,2,128]{3,1,2,0:T(8,128)(2,1)S(1)}, u32[]{:S(2)}, u32[]{:S(2)}) collective-permute-start(bf16[2,512,2,128]{3,1,2,0:T(8,128)(2,1)S(1)} %get-tuple-element.353), channel_id=1, source_target_pairs={{0,1},{1,2},{2,3},{3,4},{4,5},{5,6},{6,7},{8,9},{9,10},{10,11},{11... | collective-permute-start | bytes 1572872 | tf_op jit(solution)/shard_map/while/body/eval_jaxpr/ppermute | solution.py:11
  303.1 14.6 %collective-permute-start = (bf16[2,512,2,128]{3,1,2,0:T(8,128)(2,1)S(1)}, bf16[2,512,2,128]{3,1,2,0:T(8,128)(2,1)S(1)}, u32[]{:S(2)}, u32[]{:S(2)}) collective-permute-start(bf16[2,512,2,128]{3,1,2,0:T(8,128)(2,1)S(1)} %get-tuple-element.353), channel_id=1, source_target_pairs={{0,1},{1,2},{2,3},{3,4},{4,5},{5,6},{6,7},{8,9},{9,10},{10,11},{11... | collective-permute-start | bytes 1572872 | tf_op jit(solution)/shard_map/while/body/eval_jaxpr/ppermute | solution.py:11
  319.8 13.6 %collective-permute-start = (bf16[2,512,2,128]{3,1,2,0:T(8,128)(2,1)S(1)}, bf16[2,512,2,128]{3,1,2,0:T(8,128)(2,1)S(1)}, u32[]{:S(2)}, u32[]{:S(2)}) collective-permute-start(bf16[2,512,2,128]{3,1,2,0:T(8,128)(2,1)S(1)} %get-tuple-element.353), channel_id=1, source_target_pairs={{0,1},{1,2},{2,3},{3,4},{4,5},{5,6},{6,7},{8,9},{9,10},{10,11},{11... | collective-permute-start | bytes 1572872 | tf_op jit(solution)/shard_map/while/body/eval_jaxpr/ppermute | solution.py:11
Sparse Core Ops, SparseCore 0:
  9.2 75.5 all-gather.3
  86.6 73.6 all-gather.5
  162.1 96.1 all-gather.7
